TPU v7x, 32 devices: a whole 2x2x4 slice. The times are simulated.
32 devices in a mesh: dp: 8 (over z, y), col: 4 (over x, core).
Axes of the slice: x: 2, y: 2, z: 4, core: 2. Of those that a mesh axis runs over, the one named last changes fastest.
Arguments:
- tokens: bfloat16 [32768, 1024], P(('dp', 'col')), may hold values from -6 to 6
- cotangent: bfloat16 [32768, 1024], P(('dp', 'col')), may hold values from -6 to 6
- ln1_gain: bfloat16 [1024], replicated, may hold values from 0.5 to 1.5
- ln1_shift: bfloat16 [1024], replicated, may hold values from -1.5 to 1.5
- qkv_weight: bfloat16 [1024, 3072], replicated, may hold values from -0.1875 to 0.1875
- qkv_bias: bfloat16 [3072], replicated, may hold values from -1.5 to 1.5
- out_weight: bfloat16 [1024, 1024], replicated, may hold values from -0.75 to 0.75
- out_bias: bfloat16 [1024], replicated, may hold values from -1.5 to 1.5
- ln2_gain: bfloat16 [1024], replicated, may hold values from 0.5 to 1.5
- ln2_shift: bfloat16 [1024], replicated, may hold values from -1.5 to 1.5
- fc_weight: bfloat16 [1024, 4096], replicated, may hold values from -0.1875 to 0.1875
- fc_bias: bfloat16 [4096], replicated, may hold values from -1.5 to 1.5
- proj_weight: bfloat16 [4096, 1024], replicated, may hold values from -0.09375 to 0.09375
- proj_bias: bfloat16 [1024], replicated, may hold values from -1.5 to 1.5
- embedding: bfloat16 [10, 1024], replicated, may hold values from -6 to 6
- first_weight: bfloat16 [1024, 512], replicated, may hold values from -0.1875 to 0.1875
- first_bias: bfloat16 [512], replicated, may hold values from -1.5 to 1.5
- second_weight: bfloat16 [512, 2048], P(None, 'col'), may hold values from -0.25 to 0.25
- second_bias: bfloat16 [2048], P('col'), may hold values from -1.5 to 1.5
Outputs:
- block_out: bfloat16 [32768, 1024], P(('dp', 'col'))
- token_grad: bfloat16 [32768, 1024], P(('dp', 'col'))
- embed_grad: float32 [10, 1024], replicated
- first_grad: float32 [1024, 512], replicated
- first_bias_grad: float32 [512], replicated
- second_grad: float32 [512, 2048], P(None, 'col')
- second_bias_grad: float32 [2048], P('col')
All inputs are finite; a program needn't handle non-finite values.
Results may differ from a plain program's by a relative error of at most 0.013.
Values may be sent and summed in bfloat16 or wider, within the bound.
A program may use at most 192 MiB of HBM per device.

v0:
```python
import functools

import jax
import jax.numpy as jnp
from jax import lax
from jax.experimental import pallas as pl
from jax.experimental.pallas import tpu as pltpu
from jax.sharding import PartitionSpec as P

HEADS = 16
PREFIX = 10
PAD = 16
SEQ_LEN = 256
HALF = SEQ_LEN // 2
PAIR = 128
BLOCK = 256
FF_CHUNK = 512
FF_ROWS = 1024
GROUP = 2

EPSILON = 1e-05
MASKED = -1000000000.0
NEVER = -1e30
ROOT = 0.7978845608028654
CUBIC = 0.044715

F32 = jnp.float32
BF16 = jnp.bfloat16
NN = (((1,), (0,)), ((), ()))
NT = (((1,), (1,)), ((), ()))
TN = (((0,), (0,)), ((), ()))
MESH = pl.DeviceIdType.MESH


def dot(left, right, form=NN):
    return lax.dot_general(left, right, form, preferred_element_type=F32)


def row(ref):
    return ref[...].astype(F32).reshape(1, -1)


def normalise(values):
    average = jnp.mean(values, axis=-1, keepdims=True)
    centred = values - average
    variance = jnp.mean(centred * centred, axis=-1, keepdims=True)
    scale = lax.rsqrt(variance + EPSILON)
    return centred * scale, scale


def norm_pull(values, gain, upstream):
    unit, scale = normalise(values)
    scaled = upstream * gain
    first = jnp.mean(scaled, axis=-1, keepdims=True)
    second = jnp.mean(scaled * unit, axis=-1, keepdims=True)
    return scale * (scaled - first - unit * second)


def gelu_and_slope(values):
    square = values * values
    inner = jnp.tanh(values * (ROOT + (ROOT * CUBIC) * square))
    half = 0.5 * inner + 0.5
    bend = (0.5 - 0.5 * inner * inner) * (ROOT + (3.0 * ROOT * CUBIC) * square)
    return values * half, half + values * bend


def head_lanes():
    lane = lax.broadcasted_iota(jnp.int32, (1, PAIR), 1)
    return (lane < PAIR // 2, lane >= PAIR // 2)


def columns(base, pair):
    return pl.ds(base + pair * PAIR, PAIR)


def over_rows(row_count, group, body):
    def step(index, carry):
        for place in range(group):
            block = index * group + place
            body(block, pl.ds(pl.multiple_of(block * BLOCK, BLOCK), BLOCK))
        return carry

    lax.fori_loop(0, row_count // (BLOCK * group), step, 0)


def attention_forward(seq, width, packed, prefix, attended, top, bottom, side):
    rows = pl.ds(pl.multiple_of(seq * SEQ_LEN, SEQ_LEN), SEQ_LEN)
    pairs = width // PAIR
    key = lax.broadcasted_iota(jnp.int32, (HALF, HALF), 0)
    query = lax.broadcasted_iota(jnp.int32, (HALF, HALF), 1)
    causal = key <= query
    real = lax.broadcasted_iota(jnp.int32, (PAD, 1), 0) < PREFIX
    lanes = head_lanes()
    scores = []
    for pair in range(pairs):
        queries = packed[rows, columns(0, pair)]
        keys = packed[rows, columns(width, pair)]
        prefix_keys = prefix[:, columns(0, pair)]
        for mine in lanes:
            scores.append(
                (
                    dot(jnp.where(mine, keys, 0), queries, NT),
                    dot(jnp.where(mine, prefix_keys, 0), queries, NT),
                )
            )
    probs = []
    for full, extra in scores:
        extra = jnp.where(real, extra, NEVER)
        early = jnp.where(causal, full[:HALF, :HALF], MASKED)
        cross = full[:HALF, HALF:]
        late = jnp.where(causal, full[HALF:, HALF:], MASKED)
        peak = jnp.max(extra, axis=0, keepdims=True)
        peak_early = jnp.maximum(jnp.max(early, axis=0, keepdims=True), peak[:, :HALF])
        peak_late = jnp.maximum(
            jnp.maximum(
                jnp.max(cross, axis=0, keepdims=True), jnp.max(late, axis=0, keepdims=True)
            ),
            peak[:, HALF:],
        )
        early = jnp.exp(early - peak_early)
        cross = jnp.exp(cross - peak_late)
        late = jnp.exp(late - peak_late)
        extra = jnp.exp(extra - jnp.concatenate([peak_early, peak_late], axis=1))
        total = jnp.sum(extra, axis=0, keepdims=True)
        total_early = jnp.sum(early, axis=0, keepdims=True) + total[:, :HALF]
        total_late = (
            jnp.sum(cross, axis=0, keepdims=True)
            + jnp.sum(late, axis=0, keepdims=True)
            + total[:, HALF:]
        )
        inverse = 1.0 / jnp.concatenate([total_early, total_late], axis=1)
        first = jnp.concatenate(
            [
                (early * inverse[:, :HALF]).astype(BF16),
                (cross * inverse[:, HALF:]).astype(BF16),
            ],
            axis=1,
        )
        probs.append(
            (first, (late * inverse[:, HALF:]).astype(BF16), (extra * inverse).astype(BF16))
        )
    empty = jnp.zeros((HALF, HALF), BF16)
    for pair in range(pairs):
        values = packed[rows, columns(2 * width, pair)].T
        prefix_values = prefix[:, columns(width, pair)].T
        halves = []
        for head in (0, 1):
            first, second, extra = probs[2 * pair + head]
            place = seq * HEADS + 2 * pair + head
            top[place] = first
            bottom[place] = second
            side[place] = extra
            whole = jnp.concatenate([first, jnp.concatenate([empty, second], axis=1)], axis=0)
            mine = slice(head * (PAIR // 2), (head + 1) * (PAIR // 2))
            halves.append(dot(values[mine], whole) + dot(prefix_values[mine], extra))
        attended[rows, columns(0, pair)] = jnp.concatenate(halves, axis=0).astype(BF16).T


def attention_backward(
    seq, width, packed, prefix, upstream, attended, top, bottom, side, prefix_grad
):
    rows = pl.ds(pl.multiple_of(seq * SEQ_LEN, SEQ_LEN), SEQ_LEN)
    pairs = width // PAIR
    lanes = head_lanes()
    head_row = lax.broadcasted_iota(jnp.int32, (8, PAIR), 0)
    head_lane = lax.broadcasted_iota(jnp.int32, (8, PAIR), 1)
    picker = jnp.where(head_lane // (PAIR // 2) == head_row, 1.0, 0.0).astype(BF16)
    empty = jnp.zeros((HALF, HALF), BF16)
    incoming, deltas = [], []
    for pair in range(pairs):
        grad = upstream[rows, columns(0, pair)]
        deltas.append(dot(picker, grad * attended[rows, columns(0, pair)], NT))
        values = packed[rows, columns(2 * width, pair)]
        prefix_values = prefix[:, columns(width, pair)]
        for mine in lanes:
            incoming.append(
                (
                    dot(jnp.where(mine, values, 0), grad, NT),
                    dot(jnp.where(mine, prefix_values, 0), grad, NT),
                )
            )
    slopes = []
    for pair in range(pairs):
        for head in (0, 1):
            place = seq * HEADS + 2 * pair + head
            full, extra = incoming[2 * pair + head]
            delta = deltas[pair][head : head + 1, :]
            first = (top[place].astype(F32) * (full[:HALF] - delta)).astype(BF16)
            second = (bottom[place].astype(F32) * (full[HALF:, HALF:] - delta[:, HALF:])).astype(
                BF16
            )
            extra = (side[place].astype(F32) * (extra - delta)).astype(BF16)
            slopes.append((first, second, extra))
    for pair in range(pairs):
        grad = upstream[rows, columns(0, pair)]
        queries = packed[rows, columns(0, pair)]
        keys = packed[rows, columns(width, pair)].T
        prefix_keys = prefix[:, columns(0, pair)].T
        place = seq * HEADS + 2 * pair

        def pulled(stream, first, second, extra):
            masked = [jnp.where(mine, stream, 0) for mine in lanes]
            both = jnp.concatenate(masked, axis=0)
            late = jnp.concatenate([part[HALF:] for part in masked], axis=0)
            joined = [jnp.concatenate(part, axis=1) for part in (first, second, extra)]
            return dot(joined[0], both), dot(joined[1], late), dot(joined[2], both)

        left, right = slopes[2 * pair], slopes[2 * pair + 1]
        key_first, key_second, key_extra = pulled(
            queries, (left[0], right[0]), (left[1], right[1]), (left[2], right[2])
        )
        value_first, value_second, value_extra = pulled(
            grad,
            (top[place], top[place + 1]),
            (bottom[place], bottom[place + 1]),
            (side[place], side[place + 1]),
        )
        halves = []
        for head in (0, 1):
            first, second, extra = slopes[2 * pair + head]
            whole = jnp.concatenate([first, jnp.concatenate([empty, second], axis=1)], axis=0)
            mine = slice(head * (PAIR // 2), (head + 1) * (PAIR // 2))
            halves.append(dot(keys[mine], whole) + dot(prefix_keys[mine], extra))
        prefix_grad[:, columns(0, pair)] += key_extra
        prefix_grad[:, columns(width, pair)] += value_extra
        packed[rows, columns(0, pair)] = (
            (jnp.concatenate(halves, axis=0) * 0.125).astype(BF16).T
        )
        packed[rows, columns(width, pair)] = jnp.concatenate(
            [key_first, key_second], axis=0
        ).astype(BF16)
        packed[rows, columns(2 * width, pair)] = jnp.concatenate(
            [value_first, value_second], axis=0
        ).astype(BF16)


def layer_kernel(
    dp_size,
    col_size,
    tokens_hbm,
    cotangent_hbm,
    qkv_hbm,
    out_hbm,
    fc_hbm,
    proj_hbm,
    first_hbm,
    second_hbm,
    ln1_gain,
    ln1_shift,
    qkv_bias,
    out_bias,
    ln2_gain,
    ln2_shift,
    fc_bias,
    proj_bias,
    embedding,
    first_bias,
    second_bias,
    block_hbm,
    grad_hbm,
    hidden_out,
    owned_out,
    pre_out,
    stream,
    wide,
    out_weight,
    fc_weight,
    proj_weight,
    packed,
    top,
    bottom,
    side,
    attended,
    middle,
    normed,
    activated,
    second_weight,
    prefix,
    prefix_grad,
    padded,
    parts_col,
    parts_dp,
    parts_hidden,
    load_sem,
    store_sem,
    gather_send,
    gather_recv,
    scatter_send,
    scatter_recv,
    reduce_send,
    reduce_recv,
    hidden_send,
    hidden_recv,
):
    row_count, width = stream.shape
    ff = activated.shape[1]
    tokens = wide.at[pl.ds(0, row_count), pl.ds(3 * width, width)]
    hidden_width = second_weight.shape[0]
    owned = second_weight.shape[1]
    seqs = row_count // SEQ_LEN
    my_dp = lax.axis_index("dp")
    my_col = lax.axis_index("col")

    def col_peer(step):
        return (my_dp, lax.rem(my_col + step, col_size))

    def dp_peer(step):
        return (lax.rem(my_dp + step, dp_size), my_col)

    barrier = pltpu.get_barrier_semaphore()
    for step in range(1, col_size):
        pl.semaphore_signal(barrier, inc=1, device_id=col_peer(step), device_id_type=MESH)
    for step in range(1, dp_size):
        pl.semaphore_signal(barrier, inc=1, device_id=dp_peer(step), device_id_type=MESH)

    first_weight = activated.at[pl.ds(0, width), pl.ds(0, hidden_width)]
    thirds = [pl.ds(third * width, width) for third in range(3)]
    qkv_weight = [wide.at[pl.ds(0, width), third] for third in thirds]
    loads = [
        pltpu.make_async_copy(source, target, load_sem.at[place])
        for place, (source, target) in enumerate(
            [
                (first_hbm, first_weight),
                (second_hbm, second_weight),
                (tokens_hbm, tokens),
                (qkv_hbm.at[:, thirds[0]], qkv_weight[0]),
                (qkv_hbm.at[:, thirds[1]], qkv_weight[1]),
                (qkv_hbm.at[:, thirds[2]], qkv_weight[2]),
                (out_hbm, out_weight),
                (fc_hbm, fc_weight),
                (proj_hbm, proj_weight),
                (cotangent_hbm, stream),
            ]
        )
    ]
    for load in loads:
        load.start()

    padded[...] = jnp.zeros_like(padded)
    padded[0:PREFIX, :] = embedding[...].astype(F32)
    loads[0].wait()
    loads[1].wait()
    pre_hidden = dot(padded[...].astype(BF16), first_weight[...]) + row(first_bias)
    hidden_full = jnp.tanh(pre_hidden)
    hidden_low = hidden_full.astype(BF16)
    hidden_out[...] = hidden_low
    owned_kv = dot(hidden_low, second_weight[...]) + row(second_bias)
    mine = pl.ds(pl.multiple_of(my_col * owned, PAIR), owned)
    prefix[:, mine] = owned_kv.astype(BF16)
    pl.semaphore_wait(barrier, col_size + dp_size - 2)
    gathers = [
        pltpu.make_async_remote_copy(
            src_ref=prefix.at[:, mine],
            dst_ref=prefix.at[:, mine],
            send_sem=gather_send.at[step - 1],
            recv_sem=gather_recv.at[step - 1],
            device_id=col_peer(step),
            device_id_type=MESH,
        )
        for step in range(1, col_size)
    ]
    for gather in gathers:
        gather.start()

    loads[2].wait()
    gain_one, shift_one = row(ln1_gain), row(ln1_shift)

    def first_norm(block, rows):
        unit, _ = normalise(tokens[rows, :].astype(F32))
        normed[rows, :] = (unit * gain_one + shift_one).astype(BF16)

    over_rows(row_count, GROUP, first_norm)
    for third in range(3):
        loads[3 + third].wait()
        bias = qkv_bias[pl.ds(third * width, width)].astype(F32).reshape(1, -1)
        part = (dot(normed[...], qkv_weight[third][...]) + bias).astype(BF16)
        packed[:, thirds[third]] = part * BF16(0.125) if third == 0 else part

    for gather in gathers:
        gather.wait()

    def forward_step(seq, carry):
        attention_forward(seq, width, packed, prefix, attended, top, bottom, side)
        return carry

    lax.fori_loop(0, seqs, forward_step, 0)

    loads[6].wait()
    bias = row(out_bias)
    gain_two, shift_two = row(ln2_gain), row(ln2_shift)

    def output_rows(block, rows):
        total = tokens[rows, :].astype(F32) + dot(attended[rows, :], out_weight[...]) + bias
        middle[rows, :] = total
        unit, _ = normalise(total)
        normed[rows, :] = (unit * gain_two + shift_two).astype(BF16)

    over_rows(row_count, GROUP, output_rows)

    loads[7].wait()
    loads[8].wait()
    loads[9].wait()

    def ff_step(chunk, carry):
        units = pl.ds(pl.multiple_of(chunk * FF_CHUNK, FF_CHUNK), FF_CHUNK)
        bias = fc_bias[:, units]
        for start in range(0, row_count, FF_ROWS):
            rows = pl.ds(start, FF_ROWS)
            pre_act = dot(normed[rows, :], fc_weight[:, units]) + bias
            upstream = dot(stream[rows, :], proj_weight[units, :], NT)
            value, slope = gelu_and_slope(pre_act)
            activated[rows, units] = value.astype(BF16)
            wide[rows, units] = (slope * upstream).astype(BF16)
        return carry

    lax.fori_loop(0, ff // FF_CHUNK, ff_step, 0)

    def middle_rows(block, rows):
        upstream = dot(wide[rows, :], fc_weight[...], NT)
        total = stream[rows, :].astype(F32) + norm_pull(middle[rows, :], gain_two, upstream)
        low = total.astype(BF16)
        stream[rows, :] = low
        normed[rows, :] = dot(low, out_weight[...], NT).astype(BF16)

    over_rows(row_count, GROUP, middle_rows)

    reloads = [
        pltpu.make_async_copy(source, target, load_sem.at[2 + place])
        for place, (source, target) in enumerate(
            [(tokens_hbm, tokens)]
            + [(qkv_hbm.at[:, thirds[third]], qkv_weight[third]) for third in range(3)]
        )
    ]
    for load in reloads:
        load.start()

    prefix_grad[...] = jnp.zeros_like(prefix_grad)

    def backward_step(seq, carry):
        attention_backward(
            seq, width, packed, prefix, normed, attended, top, bottom, side, prefix_grad
        )
        return carry

    lax.fori_loop(0, seqs, backward_step, 0)

    scatters = [
        pltpu.make_async_remote_copy(
            src_ref=prefix_grad.at[
                :, pl.ds(pl.multiple_of(lax.rem(my_col + step, col_size) * owned, PAIR), owned)
            ],
            dst_ref=parts_col.at[step - 1],
            send_sem=scatter_send.at[step - 1],
            recv_sem=scatter_recv.at[step - 1],
            device_id=col_peer(step),
            device_id_type=MESH,
        )
        for step in range(1, col_size)
    ]
    reduces = [
        pltpu.make_async_remote_copy(
            src_ref=parts_dp.at[my_dp],
            dst_ref=parts_dp.at[my_dp],
            send_sem=reduce_send.at[step - 1],
            recv_sem=reduce_recv.at[step - 1],
            device_id=dp_peer(step),
            device_id_type=MESH,
        )
        for step in range(1, dp_size)
    ]
    hiddens = [
        pltpu.make_async_remote_copy(
            src_ref=parts_hidden.at[my_col],
            dst_ref=parts_hidden.at[my_col],
            send_sem=hidden_send.at[step - 1],
            recv_sem=hidden_recv.at[step - 1],
            device_id=col_peer(step),
            device_id_type=MESH,
        )
        for step in range(1, col_size)
    ]

    def exchange(stage):
        if stage == 0:
            for scatter in scatters:
                scatter.start()
        elif stage == 1:
            for scatter in scatters:
                scatter.wait()
            total = prefix_grad[:, mine]
            for step in range(1, col_size):
                total = total + parts_col[step - 1]
            parts_dp[my_dp] = total
            for reduce in reduces:
                reduce.start()
        elif stage == 2:
            for reduce in reduces:
                reduce.wait()
            total = parts_dp[0]
            for step in range(1, dp_size):
                total = total + parts_dp[step]
            low = total.astype(BF16)
            owned_out[...] = low
            parts_hidden[my_col] = dot(low, second_weight[...], NT)
            for part in hiddens:
                part.start()
        else:
            for part in hiddens:
                part.wait()
            total = parts_hidden[0]
            for step in range(1, col_size):
                total = total + parts_hidden[step]
            first_weight_sum = hidden_full * hidden_full
            pre_out[...] = (total * (1.0 - first_weight_sum)).astype(BF16)

    def store(source, target, place, rows):
        return pltpu.make_async_copy(
            source.at[rows, :], target.at[rows, :], store_sem.at[place]
        )

    blocks = row_count // BLOCK
    proj_row = row(proj_bias)
    exchange(0)

    def block_rows(block, rows):
        total = middle[rows, :] + dot(activated[rows, :], proj_weight[...]) + proj_row
        attended[rows, :] = total.astype(BF16)
        store(attended, block_hbm, block, rows).start()
        pl.when(block == 0)(lambda: exchange(1))
        pl.when(block == blocks - 2)(lambda: exchange(2))

    over_rows(row_count, 1, block_rows)
    for load in reloads:
        load.wait()

    def grad_rows(block, rows):
        upstream = dot(packed[rows, :], wide[0:width, 0 : 3 * width], NT)
        total = stream[rows, :].astype(F32) + norm_pull(
            tokens[rows, :].astype(F32), gain_one, upstream
        )
        tokens[rows, :] = total.astype(BF16)
        store(tokens, grad_hbm, blocks + block, rows).start()

    over_rows(row_count, GROUP, grad_rows)
    exchange(3)
    for block in range(blocks):
        rows = pl.ds(block * BLOCK, BLOCK)
        store(attended, block_hbm, block, rows).wait()
        store(tokens, grad_hbm, blocks + block, rows).wait()


def small_kernel(
    embedding, first_weight, hidden, owned, pre, embed_grad, first_grad, first_bias_grad,
    second_grad, second_bias_grad, padded
):
    padded[...] = jnp.zeros_like(padded)
    padded[0:PREFIX, :] = embedding[...].astype(F32)
    low = padded[...].astype(BF16)
    first_grad[...] = dot(low, pre[...], TN)
    second_grad[...] = dot(hidden[...], owned[...], TN)
    embed_grad[...] = dot(pre[...], first_weight[...], NT)[:PREFIX]
    first_bias_grad[...] = jnp.sum(pre[...].astype(F32), axis=0)
    second_bias_grad[...] = jnp.sum(owned[...].astype(F32), axis=0)


def shards(
    dp_size,
    col_size,
    tokens,
    cotangent,
    ln1_gain,
    ln1_shift,
    qkv_weight,
    qkv_bias,
    out_weight,
    out_bias,
    ln2_gain,
    ln2_shift,
    fc_weight,
    fc_bias,
    proj_weight,
    proj_bias,
    embedding,
    first_weight,
    first_bias,
    second_weight,
    second_bias,
):
    row_count, width = tokens.shape
    ff = fc_weight.shape[1]
    hidden_width, owned = second_weight.shape
    heads = row_count // SEQ_LEN * HEADS
    anywhere = pl.BlockSpec(memory_space=pl.ANY)
    local = pl.BlockSpec(memory_space=pltpu.VMEM)
    dma = pltpu.SemaphoreType.DMA
    block_out, token_grad, hidden, owned_grad, pre_grad = pl.pallas_call(
        functools.partial(layer_kernel, dp_size, col_size),
        out_shape=(
            jax.ShapeDtypeStruct((row_count, width), BF16),
            jax.ShapeDtypeStruct((row_count, width), BF16),
            jax.ShapeDtypeStruct((PAD, hidden_width), BF16),
            jax.ShapeDtypeStruct((PAD, owned), BF16),
            jax.ShapeDtypeStruct((PAD, hidden_width), BF16),
        ),
        in_specs=[anywhere] * 8 + [local] * 11,
        out_specs=[anywhere] * 2 + [local] * 3,
        scratch_shapes=[
            pltpu.VMEM((row_count, width), BF16),
            pltpu.VMEM((max(row_count, width), ff), BF16),
            pltpu.VMEM((width, width), BF16),
            pltpu.VMEM((width, ff), BF16),
            pltpu.VMEM((ff, width), BF16),
            pltpu.VMEM((row_count, 3 * width), BF16),
            pltpu.VMEM((heads, HALF, SEQ_LEN), BF16),
            pltpu.VMEM((heads, HALF, HALF), BF16),
            pltpu.VMEM((heads, PAD, SEQ_LEN), BF16),
            pltpu.VMEM((row_count, width), BF16),
            pltpu.VMEM((row_count, width), F32),
            pltpu.VMEM((row_count, width), BF16),
            pltpu.VMEM((max(row_count, width), ff), BF16),
            pltpu.VMEM((hidden_width, owned), BF16),
            pltpu.VMEM((PAD, col_size * owned), BF16),
            pltpu.VMEM((PAD, col_size * owned), F32),
            pltpu.VMEM((PAD, width), F32),
            pltpu.VMEM((col_size - 1, PAD, owned), F32),
            pltpu.VMEM((dp_size, PAD, owned), F32),
            pltpu.VMEM((col_size, PAD, hidden_width), F32),
            dma((10,)),
            dma((2 * (row_count // BLOCK),)),
            dma((col_size - 1,)),
            dma((col_size - 1,)),
            dma((col_size - 1,)),
            dma((col_size - 1,)),
            dma((dp_size - 1,)),
            dma((dp_size - 1,)),
            dma((col_size - 1,)),
            dma((col_size - 1,)),
        ],
        compiler_params=pltpu.CompilerParams(
            collective_id=0, has_side_effects=True, vmem_limit_bytes=63 * 2**20
        ),
        name="layer",
    )(
        tokens,
        cotangent,
        qkv_weight,
        out_weight,
        fc_weight,
        proj_weight,
        first_weight,
        second_weight,
        ln1_gain,
        ln1_shift,
        qkv_bias,
        out_bias,
        ln2_gain,
        ln2_shift,
        fc_bias.astype(F32).reshape(1, -1),
        proj_bias,
        embedding,
        first_bias,
        second_bias,
    )
    embed_grad, first_grad, first_bias_grad, second_grad, second_bias_grad = pl.pallas_call(
        small_kernel,
        out_shape=(
            jax.ShapeDtypeStruct((PREFIX, width), F32),
            jax.ShapeDtypeStruct((width, hidden_width), F32),
            jax.ShapeDtypeStruct((hidden_width,), F32),
            jax.ShapeDtypeStruct((hidden_width, owned), F32),
            jax.ShapeDtypeStruct((owned,), F32),
        ),
        in_specs=[local] * 5,
        out_specs=[local] * 5,
        scratch_shapes=[pltpu.VMEM((PAD, width), F32)],
        name="small_grads",
    )(embedding, first_weight, hidden, owned_grad, pre_grad)
    return (
        block_out,
        token_grad,
        embed_grad,
        first_grad,
        first_bias_grad,
        second_grad,
        second_bias_grad,
    )


def solution(mesh):
    placed = (
        P(("dp", "col"), None),
        P(("dp", "col"), None),
        P(),
        P(),
        P(),
        P(),
        P(),
        P(),
        P(),
        P(),
        P(),
        P(),
        P(),
        P(),
        P(),
        P(),
        P(),
        P(None, "col"),
        P("col"),
    )
    return jax.shard_map(
        functools.partial(shards, mesh.shape["dp"], mesh.shape["col"]),
        mesh=mesh,
        in_specs=placed,
        out_specs=(
            P(("dp", "col"), None),
            P(("dp", "col"), None),
            P(),
            P(),
            P(),
            P(None, "col"),
            P("col"),
        ),
        check_vma=False,
    )
```

profile of v0, /device:TPU:0, one launch (start us, length us, event | category | flops | bytes accessed | tf_op | source)
XLA Modules:
  0.0 100.7 jit_solution(12529952704823684785)
XLA Ops:
  0.6 1.3 %reshape.21 = f32[4096]{0:T(1024)} convert(bf16[4096]{0:T(1024)(128)(2,1)} %param.30) | non-fusion elementwise | flops 4096 | bytes 24576 | tf_op jit(solution)/shard_map/reshape | solution.py:658
  1.9 90.9 %layer.1 = (bf16[1024,1024]{1,0:T(8,128)(2,1)}, bf16[1024,1024]{1,0:T(8,128)(2,1)}, bf16[16,512]{1,0:T(8,128)(2,1)}, bf16[16,512]{1,0:T(8,128)(2,1)}, bf16[16,512]{1,0:T(8,128)(2,1)}) custom-call(bf16[1024,1024]{1,0:T(8,128)(2,1)} %tokens_hbm.1, bf16[1024,1024]{1,0:T(8,128)(2,1)} %cotangent_hbm.1, bf16[1024,3072]{1,0:T(8,128)(2,1)} %qkv_hbm.1, ...), custom_call_target="tpu_custom_call" | custom-call | tf_op jit(solution)/shard_map/layer/pallas_call | solution.py:596
  92.8 3.4 %small_grads.1 = (f32[10,1024]{1,0:T(8,128)}, f32[1024,512]{1,0:T(8,128)}, f32[512]{0:T(512)}, f32[512,512]{1,0:T(8,128)}, f32[512]{0:T(512)}) custom-call(bf16[10,1024]{1,0:T(8,128)(2,1)} %embedding.3, bf16[1024,512]{1,0:T(8,128)(2,1)} %first_weight.1, bf16[16,512]{1,0:T(8,128)(2,1)} %get-tuple-element.19.hidden, bf16[16,512]{1,0:T(8,128)(2,1)} %get-tuple-element.20.owned, ...), custom_call_target="tpu_custom_call" | custom-call | tf_op jit(solution)/shard_map/small_grads/pallas_call | solution.py:664
  96.2 0.0 copy-start
  96.2 3.2 %copy.28 = bf16[1024,1024]{1,0:T(8,128)(2,1)} copy(bf16[1024,1024]{1,0:T(8,128)(2,1)} %get-tuple-element.34) | data formatting | bytes 4194304
  99.4 0.0 copy-done
  99.4 1.3 %copy.29 = bf16[1024,1024]{1,0:T(8,128)(2,1)} copy(bf16[1024,1024]{1,0:T(8,128)(2,1)S(1)} %copy-done) | data formatting | bytes 4194304
Async XLA Ops:
  96.2 3.2 %copy-start = (bf16[1024,1024]{1,0:T(8,128)(2,1)S(1)}, bf16[1024,1024]{1,0:T(8,128)(2,1)}, u32[]{:S(2)}) copy-start(bf16[1024,1024]{1,0:T(8,128)(2,1)} %get-tuple-element.35) | copy-start | bytes 6291460
where the time goes:
time: 101 us
  Pallas kernels  94.2 us (93%)
  local copies, waits for them, and re-layouts  4.55 us (5%)
  other arithmetic  1.3 us (1%)
    pallas_call x1, Pallas kernels, shards(): pl.pallas_call(functools.partial(layer_kernel, dp_size, col_size), out_sh...  90.9 us
    unnamed x4, local copies, waits for them, and re-layouts  4.55 us
    pallas_call x1, Pallas kernels, shards(): pl.pallas_call(small_kernel, out_shape=(jax.ShapeDtypeStruct((PREFIX, wid...  3.37 us

commit v1 on v0

--- a/solution.py
+++ b/solution.py
@@ -256,12 +256,12 @@
     embedding,
     first_bias,
     second_bias,
-    block_hbm,
-    grad_hbm,
+    attended,
+    stream,
     hidden_out,
     owned_out,
     pre_out,
-    stream,
+    embed_out,
     wide,
     out_weight,
     fc_weight,
@@ -270,7 +270,6 @@
     top,
     bottom,
     side,
-    attended,
     middle,
     normed,
     activated,
@@ -278,11 +277,11 @@
     prefix,
     prefix_grad,
     padded,
+    ff_bias,
     parts_col,
     parts_dp,
     parts_hidden,
     load_sem,
-    store_sem,
     gather_send,
     gather_recv,
     scatter_send,
@@ -316,16 +315,15 @@
     first_weight = activated.at[pl.ds(0, width), pl.ds(0, hidden_width)]
     thirds = [pl.ds(third * width, width) for third in range(3)]
     qkv_weight = [wide.at[pl.ds(0, width), third] for third in thirds]
+    blocks = row_count // BLOCK
+    block_rows = [pl.ds(block * BLOCK, BLOCK) for block in range(blocks)]
     loads = [
         pltpu.make_async_copy(source, target, load_sem.at[place])
         for place, (source, target) in enumerate(
-            [
-                (first_hbm, first_weight),
-                (second_hbm, second_weight),
-                (tokens_hbm, tokens),
-                (qkv_hbm.at[:, thirds[0]], qkv_weight[0]),
-                (qkv_hbm.at[:, thirds[1]], qkv_weight[1]),
-                (qkv_hbm.at[:, thirds[2]], qkv_weight[2]),
+            [(tokens_hbm.at[rows, :], tokens.at[rows, :]) for rows in block_rows]
+            + [(first_hbm, first_weight), (second_hbm, second_weight)]
+            + [(qkv_hbm.at[:, thirds[third]], qkv_weight[third]) for third in range(3)]
+            + [
                 (out_hbm, out_weight),
                 (fc_hbm, fc_weight),
                 (proj_hbm, proj_weight),
@@ -335,19 +333,28 @@
     ]
     for load in loads:
         load.start()
+    token_loads, loads = loads[:blocks], loads[blocks:]
 
     padded[...] = jnp.zeros_like(padded)
     padded[0:PREFIX, :] = embedding[...].astype(F32)
+    ff_bias[...] = row(fc_bias)
+
+    gain_one, shift_one = row(ln1_gain), row(ln1_shift)
+    for load, rows in zip(token_loads, block_rows):
+        load.wait()
+        unit, _ = normalise(tokens[rows, :].astype(F32))
+        normed[rows, :] = (unit * gain_one + shift_one).astype(BF16)
+
     loads[0].wait()
     loads[1].wait()
-    pre_hidden = dot(padded[...].astype(BF16), first_weight[...]) + row(first_bias)
+    embed_out[...] = padded[...].astype(BF16)
+    pre_hidden = dot(embed_out[...], first_weight[...]) + row(first_bias)
     hidden_full = jnp.tanh(pre_hidden)
     hidden_low = hidden_full.astype(BF16)
     hidden_out[...] = hidden_low
     owned_kv = dot(hidden_low, second_weight[...]) + row(second_bias)
     mine = pl.ds(pl.multiple_of(my_col * owned, PAIR), owned)
     prefix[:, mine] = owned_kv.astype(BF16)
-    pl.semaphore_wait(barrier, col_size + dp_size - 2)
     gathers = [
         pltpu.make_async_remote_copy(
             src_ref=prefix.at[:, mine],
@@ -359,22 +366,16 @@
         )
         for step in range(1, col_size)
     ]
-    for gather in gathers:
-        gather.start()
-
-    loads[2].wait()
-    gain_one, shift_one = row(ln1_gain), row(ln1_shift)
-
-    def first_norm(block, rows):
-        unit, _ = normalise(tokens[rows, :].astype(F32))
-        normed[rows, :] = (unit * gain_one + shift_one).astype(BF16)
-
-    over_rows(row_count, GROUP, first_norm)
+
     for third in range(3):
-        loads[3 + third].wait()
+        loads[2 + third].wait()
         bias = qkv_bias[pl.ds(third * width, width)].astype(F32).reshape(1, -1)
         part = (dot(normed[...], qkv_weight[third][...]) + bias).astype(BF16)
         packed[:, thirds[third]] = part * BF16(0.125) if third == 0 else part
+        if third == 0:
+            pl.semaphore_wait(barrier, col_size + dp_size - 2)
+            for gather in gathers:
+                gather.start()
 
     for gather in gathers:
         gather.wait()
@@ -385,25 +386,24 @@
 
     lax.fori_loop(0, seqs, forward_step, 0)
 
-    loads[6].wait()
+    loads[5].wait()
     bias = row(out_bias)
     gain_two, shift_two = row(ln2_gain), row(ln2_shift)
 
     def output_rows(block, rows):
         total = tokens[rows, :].astype(F32) + dot(attended[rows, :], out_weight[...]) + bias
-        middle[rows, :] = total
+        middle[rows, :] = total.astype(BF16)
         unit, _ = normalise(total)
         normed[rows, :] = (unit * gain_two + shift_two).astype(BF16)
 
     over_rows(row_count, GROUP, output_rows)
 
-    loads[7].wait()
-    loads[8].wait()
-    loads[9].wait()
+    for load in loads[6:]:
+        load.wait()
 
     def ff_step(chunk, carry):
         units = pl.ds(pl.multiple_of(chunk * FF_CHUNK, FF_CHUNK), FF_CHUNK)
-        bias = fc_bias[:, units]
+        bias = ff_bias[:, units]
         for start in range(0, row_count, FF_ROWS):
             rows = pl.ds(start, FF_ROWS)
             pre_act = dot(normed[rows, :], fc_weight[:, units]) + bias
@@ -417,7 +417,9 @@
 
     def middle_rows(block, rows):
         upstream = dot(wide[rows, :], fc_weight[...], NT)
-        total = stream[rows, :].astype(F32) + norm_pull(middle[rows, :], gain_two, upstream)
+        total = stream[rows, :].astype(F32) + norm_pull(
+            middle[rows, :].astype(F32), gain_two, upstream
+        )
         low = total.astype(BF16)
         stream[rows, :] = low
         normed[rows, :] = dot(low, out_weight[...], NT).astype(BF16)
@@ -425,7 +427,7 @@
     over_rows(row_count, GROUP, middle_rows)
 
     reloads = [
-        pltpu.make_async_copy(source, target, load_sem.at[2 + place])
+        pltpu.make_async_copy(source, target, load_sem.at[place])
         for place, (source, target) in enumerate(
             [(tokens_hbm, tokens)]
             + [(qkv_hbm.at[:, thirds[third]], qkv_weight[third]) for third in range(3)]
@@ -513,23 +515,15 @@
             first_weight_sum = hidden_full * hidden_full
             pre_out[...] = (total * (1.0 - first_weight_sum)).astype(BF16)
 
-    def store(source, target, place, rows):
-        return pltpu.make_async_copy(
-            source.at[rows, :], target.at[rows, :], store_sem.at[place]
-        )
-
-    blocks = row_count // BLOCK
+    exchange(0)
     proj_row = row(proj_bias)
-    exchange(0)
-
-    def block_rows(block, rows):
-        total = middle[rows, :] + dot(activated[rows, :], proj_weight[...]) + proj_row
+
+    def proj_rows(block, rows):
+        total = middle[rows, :].astype(F32) + dot(activated[rows, :], proj_weight[...]) + proj_row
         attended[rows, :] = total.astype(BF16)
-        store(attended, block_hbm, block, rows).start()
-        pl.when(block == 0)(lambda: exchange(1))
-        pl.when(block == blocks - 2)(lambda: exchange(2))
-
-    over_rows(row_count, 1, block_rows)
+        pl.when(block == 1)(lambda: exchange(1))
+
+    over_rows(row_count, 1, proj_rows)
     for load in reloads:
         load.wait()
 
@@ -538,29 +532,57 @@
         total = stream[rows, :].astype(F32) + norm_pull(
             tokens[rows, :].astype(F32), gain_one, upstream
         )
-        tokens[rows, :] = total.astype(BF16)
-        store(tokens, grad_hbm, blocks + block, rows).start()
-
-    over_rows(row_count, GROUP, grad_rows)
+        stream[rows, :] = total.astype(BF16)
+        pl.when(block == 1)(lambda: exchange(2))
+
+    over_rows(row_count, 2, grad_rows)
     exchange(3)
-    for block in range(blocks):
-        rows = pl.ds(block * BLOCK, BLOCK)
-        store(attended, block_hbm, block, rows).wait()
-        store(tokens, grad_hbm, blocks + block, rows).wait()
-
 
 def small_kernel(
-    embedding, first_weight, hidden, owned, pre, embed_grad, first_grad, first_bias_grad,
-    second_grad, second_bias_grad, padded
+    block_in,
+    grad_in,
+    hidden,
+    owned,
+    pre,
+    embedding,
+    first_hbm,
+    block_out,
+    grad_out,
+    embed_grad,
+    first_out,
+    first_bias_grad,
+    second_out,
+    second_bias_grad,
+    first_weight,
+    first_grad,
+    second_grad,
+    sem,
 ):
-    padded[...] = jnp.zeros_like(padded)
-    padded[0:PREFIX, :] = embedding[...].astype(F32)
-    low = padded[...].astype(BF16)
-    first_grad[...] = dot(low, pre[...], TN)
+    load = pltpu.make_async_copy(first_hbm, first_weight, sem.at[0])
+    writes = [
+        pltpu.make_async_copy(source, target, sem.at[1 + place])
+        for place, (source, target) in enumerate(
+            [
+                (first_grad, first_out),
+                (second_grad, second_out),
+                (block_in, block_out),
+                (grad_in, grad_out),
+            ]
+        )
+    ]
+    load.start()
+    writes[2].start()
+    writes[3].start()
     second_grad[...] = dot(hidden[...], owned[...], TN)
-    embed_grad[...] = dot(pre[...], first_weight[...], NT)[:PREFIX]
+    writes[1].start()
+    first_grad[...] = dot(embedding[...], pre[...], TN)
+    writes[0].start()
     first_bias_grad[...] = jnp.sum(pre[...].astype(F32), axis=0)
     second_bias_grad[...] = jnp.sum(owned[...].astype(F32), axis=0)
+    load.wait()
+    embed_grad[...] = dot(pre[...], first_weight[...], NT)[:PREFIX]
+    for write in writes:
+        write.wait()
 
 
 def shards(
@@ -593,19 +615,19 @@
     anywhere = pl.BlockSpec(memory_space=pl.ANY)
     local = pl.BlockSpec(memory_space=pltpu.VMEM)
     dma = pltpu.SemaphoreType.DMA
-    block_out, token_grad, hidden, owned_grad, pre_grad = pl.pallas_call(
+    results = pl.pallas_call(
         functools.partial(layer_kernel, dp_size, col_size),
         out_shape=(
-            jax.ShapeDtypeStruct((row_count, width), BF16),
-            jax.ShapeDtypeStruct((row_count, width), BF16),
-            jax.ShapeDtypeStruct((PAD, hidden_width), BF16),
-            jax.ShapeDtypeStruct((PAD, owned), BF16),
-            jax.ShapeDtypeStruct((PAD, hidden_width), BF16),
+            pltpu.VMEM((row_count, width), BF16),
+            pltpu.VMEM((row_count, width), BF16),
+            pltpu.VMEM((PAD, hidden_width), BF16),
+            pltpu.VMEM((PAD, owned), BF16),
+            pltpu.VMEM((PAD, hidden_width), BF16),
+            pltpu.VMEM((PAD, width), BF16),
         ),
         in_specs=[anywhere] * 8 + [local] * 11,
-        out_specs=[anywhere] * 2 + [local] * 3,
+        out_specs=[local] * 6,
         scratch_shapes=[
-            pltpu.VMEM((row_count, width), BF16),
             pltpu.VMEM((max(row_count, width), ff), BF16),
             pltpu.VMEM((width, width), BF16),
             pltpu.VMEM((width, ff), BF16),
@@ -615,18 +637,17 @@
             pltpu.VMEM((heads, HALF, HALF), BF16),
             pltpu.VMEM((heads, PAD, SEQ_LEN), BF16),
             pltpu.VMEM((row_count, width), BF16),
-            pltpu.VMEM((row_count, width), F32),
             pltpu.VMEM((row_count, width), BF16),
             pltpu.VMEM((max(row_count, width), ff), BF16),
             pltpu.VMEM((hidden_width, owned), BF16),
             pltpu.VMEM((PAD, col_size * owned), BF16),
             pltpu.VMEM((PAD, col_size * owned), F32),
             pltpu.VMEM((PAD, width), F32),
+            pltpu.VMEM((1, ff), F32),
             pltpu.VMEM((col_size - 1, PAD, owned), F32),
             pltpu.VMEM((dp_size, PAD, owned), F32),
             pltpu.VMEM((col_size, PAD, hidden_width), F32),
-            dma((10,)),
-            dma((2 * (row_count // BLOCK),)),
+            dma((9 + row_count // BLOCK,)),
             dma((col_size - 1,)),
             dma((col_size - 1,)),
             dma((col_size - 1,)),
@@ -637,7 +658,7 @@
             dma((col_size - 1,)),
         ],
         compiler_params=pltpu.CompilerParams(
-            collective_id=0, has_side_effects=True, vmem_limit_bytes=63 * 2**20
+            collective_id=0, has_side_effects=True, vmem_limit_bytes=239 * 2**18
         ),
         name="layer",
     )(
@@ -655,35 +676,35 @@
         out_bias,
         ln2_gain,
         ln2_shift,
-        fc_bias.astype(F32).reshape(1, -1),
+        fc_bias,
         proj_bias,
         embedding,
         first_bias,
         second_bias,
     )
-    embed_grad, first_grad, first_bias_grad, second_grad, second_bias_grad = pl.pallas_call(
+    held = [pltpu.with_memory_space_constraint(result, pltpu.VMEM) for result in results]
+    return pl.pallas_call(
         small_kernel,
         out_shape=(
+            jax.ShapeDtypeStruct((row_count, width), BF16),
+            jax.ShapeDtypeStruct((row_count, width), BF16),
             jax.ShapeDtypeStruct((PREFIX, width), F32),
             jax.ShapeDtypeStruct((width, hidden_width), F32),
             jax.ShapeDtypeStruct((hidden_width,), F32),
             jax.ShapeDtypeStruct((hidden_width, owned), F32),
             jax.ShapeDtypeStruct((owned,), F32),
         ),
-        in_specs=[local] * 5,
-        out_specs=[local] * 5,
-        scratch_shapes=[pltpu.VMEM((PAD, width), F32)],
+        in_specs=[local] * 6 + [anywhere],
+        out_specs=[anywhere, anywhere, local, anywhere, local, anywhere, local],
+        scratch_shapes=[
+            pltpu.VMEM((width, hidden_width), BF16),
+            pltpu.VMEM((width, hidden_width), F32),
+            pltpu.VMEM((hidden_width, owned), F32),
+            dma((5,)),
+        ],
+        compiler_params=pltpu.CompilerParams(vmem_limit_bytes=16 * 2**20),
         name="small_grads",
-    )(embedding, first_weight, hidden, owned_grad, pre_grad)
-    return (
-        block_out,
-        token_grad,
-        embed_grad,
-        first_grad,
-        first_bias_grad,
-        second_grad,
-        second_bias_grad,
-    )
+    )(*held, first_weight)
 
 
 def solution(mesh):

time: 101 us -> 89.7 us (0.89)
  Pallas kernels: 94.2 us -> 87.4 us
  local copies, waits for them, and re-layouts: 4.55 us -> 1.22 us
  other arithmetic: 1.3 us -> 0 us
    pallas_call x1, Pallas kernels: 90.9 us -> 83.7 us  [shards(): pl.pallas_call(functools.partial(layer_kernel, dp_size, col_size), out_sh...]
    unnamed x4 -> x2, local copies, waits for them, and re-layouts: 4.55 us -> 1.22 us
    reshape x1 -> x0, other arithmetic: 1.3 us -> none  [shards(): fc_bias.astype(F32).reshape(1, -1)]
where the time goes in v1:
time: 89.7 us; the launch traced here: 89.5 us
  Pallas kernels  87.4 us (97%)
  local copies, waits for them, and re-layouts  1.22 us (1%)
    pallas_call x1, Pallas kernels, shards(): pl.pallas_call(functools.partial(layer_kernel, dp_size, col_size), out_sh...  83.7 us
    pallas_call x1, Pallas kernels, shards(): pl.pallas_call(small_kernel, out_shape=(jax.ShapeDtypeStruct((row_count,...  3.77 us

profile of v1, /device:TPU:0, one launch (start us, length us, event | category | flops | bytes accessed | tf_op | source)
XLA Modules:
  0.0 89.5 jit_solution(1403153174946866175)
XLA Ops:
  0.6 83.7 %layer.1 = (bf16[1024,1024]{1,0:T(8,128)(2,1)S(1)}, bf16[1024,1024]{1,0:T(8,128)(2,1)S(1)}, bf16[16,512]{1,0:T(8,128)(2,1)S(1)}, bf16[16,512]{1,0:T(8,128)(2,1)S...) custom-call(bf16[1024,1024]{1,0:T(8,128)(2,1)} %tokens_hbm.1, bf16[1024,1024]{1,0:T(8,128)(2,1)} %cotangent_hbm.1, ...), custom_call_target="tpu_custom_call" | custom-call | tf_op jit(solution)/shard_map/layer/pallas_call | solution.py:618
  84.3 0.0 copy-start
  84.3 1.2 %copy-done = bf16[1024,512]{1,0:T(8,128)(2,1)S(1)} copy-done((bf16[1024,512]{1,0:T(8,128)(2,1)S(1)}, bf16[1024,512]{1,0:T(8,128)(2,1)}, u32[]{:S(2)}) %copy-start) | copy-done | bytes 1048600
  85.6 3.8 %small_grads.1 = (bf16[1024,1024]{1,0:T(8,128)(2,1)}, bf16[1024,1024]{1,0:T(8,128)(2,1)}, f32[10,1024]{1,0:T(8,128)}, f32[1024,512]{1,0:T(8,128)}, f32[512]{0:T(512)}, /*index=5*/f32[512,512]{1,0:T(8,128)}, f32[512]{0:T(512)}) custom-call(bf16[1024,1024]{1,0:T(8,128)(2,1)S(1)} %get-tuple-element.13.block_in, ...), custom_call_target="tpu_custom_call" | custom-call | tf_op jit(solution)/shard_map/small_grads/pallas_call | solution.py:686
Async XLA Ops:
  84.3 1.2 %copy-start = (bf16[1024,512]{1,0:T(8,128)(2,1)S(1)}, bf16[1024,512]{1,0:T(8,128)(2,1)}, u32[]{:S(2)}) copy-start(bf16[1024,512]{1,0:T(8,128)(2,1)} %first_hbm.3) | copy-start | bytes 3145732

commit v2 on v1

--- a/solution.py
+++ b/solution.py
@@ -40,20 +40,24 @@
     return ref[...].astype(F32).reshape(1, -1)
 
 
-def normalise(values):
+def centre(values):
     average = jnp.mean(values, axis=-1, keepdims=True)
     centred = values - average
     variance = jnp.mean(centred * centred, axis=-1, keepdims=True)
-    scale = lax.rsqrt(variance + EPSILON)
-    return centred * scale, scale
+    return centred, lax.rsqrt(variance + EPSILON)
+
+
+def normalise(values):
+    centred, scale = centre(values)
+    return centred * scale
 
 
 def norm_pull(values, gain, upstream):
-    unit, scale = normalise(values)
+    centred, scale = centre(values)
     scaled = upstream * gain
     first = jnp.mean(scaled, axis=-1, keepdims=True)
-    second = jnp.mean(scaled * unit, axis=-1, keepdims=True)
-    return scale * (scaled - first - unit * second)
+    second = jnp.mean(scaled * centred, axis=-1, keepdims=True)
+    return (scaled - first) * scale - centred * (scale * scale * scale * second)
 
 
 def gelu_and_slope(values):
@@ -81,6 +85,22 @@
         return carry
 
     lax.fori_loop(0, row_count // (BLOCK * group), step, 0)
+
+
+def pair_products(mine, prefix, others, lanes):
+    stacked = [jnp.where(lane, mine[:HALF], 0) for lane in lanes]
+    stacked += [jnp.where(lane, prefix, 0) for lane in lanes]
+    late = jnp.concatenate([jnp.where(lane, others[HALF:], 0) for lane in lanes], axis=0)
+    second = dot(mine[HALF:], late, NT)
+    rest = dot(jnp.concatenate(stacked, axis=0), others, NT)
+    return [
+        (
+            rest[head * HALF : (head + 1) * HALF],
+            second[:, head * HALF : (head + 1) * HALF],
+            rest[2 * HALF + head * PAD : 2 * HALF + (head + 1) * PAD],
+        )
+        for head in (0, 1)
+    ]
 
 
 def attention_forward(seq, width, packed, prefix, attended, top, bottom, side):
@@ -93,22 +113,18 @@
     lanes = head_lanes()
     scores = []
     for pair in range(pairs):
-        queries = packed[rows, columns(0, pair)]
-        keys = packed[rows, columns(width, pair)]
-        prefix_keys = prefix[:, columns(0, pair)]
-        for mine in lanes:
-            scores.append(
-                (
-                    dot(jnp.where(mine, keys, 0), queries, NT),
-                    dot(jnp.where(mine, prefix_keys, 0), queries, NT),
-                )
-            )
+        scores += pair_products(
+            packed[rows, columns(width, pair)],
+            prefix[:, columns(0, pair)],
+            packed[rows, columns(0, pair)],
+            lanes,
+        )
     probs = []
-    for full, extra in scores:
+    for first, second, extra in scores:
         extra = jnp.where(real, extra, NEVER)
-        early = jnp.where(causal, full[:HALF, :HALF], MASKED)
-        cross = full[:HALF, HALF:]
-        late = jnp.where(causal, full[HALF:, HALF:], MASKED)
+        early = jnp.where(causal, first[:, :HALF], MASKED)
+        cross = first[:, HALF:]
+        late = jnp.where(causal, second, MASKED)
         peak = jnp.max(extra, axis=0, keepdims=True)
         peak_early = jnp.maximum(jnp.max(early, axis=0, keepdims=True), peak[:, :HALF])
         peak_late = jnp.maximum(
@@ -170,25 +186,19 @@
     for pair in range(pairs):
         grad = upstream[rows, columns(0, pair)]
         deltas.append(dot(picker, grad * attended[rows, columns(0, pair)], NT))
-        values = packed[rows, columns(2 * width, pair)]
-        prefix_values = prefix[:, columns(width, pair)]
-        for mine in lanes:
-            incoming.append(
-                (
-                    dot(jnp.where(mine, values, 0), grad, NT),
-                    dot(jnp.where(mine, prefix_values, 0), grad, NT),
-                )
+        incoming.append(
+            pair_products(
+                packed[rows, columns(2 * width, pair)], prefix[:, columns(width, pair)], grad, lanes
             )
+        )
     slopes = []
     for pair in range(pairs):
         for head in (0, 1):
             place = seq * HEADS + 2 * pair + head
-            full, extra = incoming[2 * pair + head]
+            first, second, extra = incoming[pair][head]
             delta = deltas[pair][head : head + 1, :]
-            first = (top[place].astype(F32) * (full[:HALF] - delta)).astype(BF16)
-            second = (bottom[place].astype(F32) * (full[HALF:, HALF:] - delta[:, HALF:])).astype(
-                BF16
-            )
+            first = (top[place].astype(F32) * (first - delta)).astype(BF16)
+            second = (bottom[place].astype(F32) * (second - delta[:, HALF:])).astype(BF16)
             extra = (side[place].astype(F32) * (extra - delta)).astype(BF16)
             slopes.append((first, second, extra))
     for pair in range(pairs):
@@ -202,8 +212,10 @@
             masked = [jnp.where(mine, stream, 0) for mine in lanes]
             both = jnp.concatenate(masked, axis=0)
             late = jnp.concatenate([part[HALF:] for part in masked], axis=0)
-            joined = [jnp.concatenate(part, axis=1) for part in (first, second, extra)]
-            return dot(joined[0], both), dot(joined[1], late), dot(joined[2], both)
+            joined = [jnp.concatenate(part, axis=1) for part in (first, second)]
+            beside = dot(jnp.concatenate(extra, axis=0), stream)
+            beside = jnp.where(lanes[0], beside[:PAD], beside[PAD:])
+            return dot(joined[0], both), dot(joined[1], late), beside
 
         left, right = slopes[2 * pair], slopes[2 * pair + 1]
         key_first, key_second, key_extra = pulled(
@@ -342,7 +354,7 @@
     gain_one, shift_one = row(ln1_gain), row(ln1_shift)
     for load, rows in zip(token_loads, block_rows):
         load.wait()
-        unit, _ = normalise(tokens[rows, :].astype(F32))
+        unit = normalise(tokens[rows, :].astype(F32))
         normed[rows, :] = (unit * gain_one + shift_one).astype(BF16)
 
     loads[0].wait()
@@ -393,10 +405,10 @@
     def output_rows(block, rows):
         total = tokens[rows, :].astype(F32) + dot(attended[rows, :], out_weight[...]) + bias
         middle[rows, :] = total.astype(BF16)
-        unit, _ = normalise(total)
+        unit = normalise(total)
         normed[rows, :] = (unit * gain_two + shift_two).astype(BF16)
 
-    over_rows(row_count, GROUP, output_rows)
+    over_rows(row_count, 4, output_rows)
 
     for load in loads[6:]:
         load.wait()
@@ -424,7 +436,7 @@
         stream[rows, :] = low
         normed[rows, :] = dot(low, out_weight[...], NT).astype(BF16)
 
-    over_rows(row_count, GROUP, middle_rows)
+    over_rows(row_count, 4, middle_rows)
 
     reloads = [
         pltpu.make_async_copy(source, target, load_sem.at[place])
@@ -523,7 +535,7 @@
         attended[rows, :] = total.astype(BF16)
         pl.when(block == 1)(lambda: exchange(1))
 
-    over_rows(row_count, 1, proj_rows)
+    over_rows(row_count, 2, proj_rows)
     for load in reloads:
         load.wait()
 
@@ -548,14 +560,17 @@
     first_hbm,
     block_out,
     grad_out,
-    embed_grad,
+    embed_out,
     first_out,
-    first_bias_grad,
+    first_bias_out,
     second_out,
-    second_bias_grad,
+    second_bias_out,
     first_weight,
     first_grad,
     second_grad,
+    first_bias_grad,
+    second_bias_grad,
+    embed_grad,
     sem,
 ):
     load = pltpu.make_async_copy(first_hbm, first_weight, sem.at[0])
@@ -563,24 +578,30 @@
         pltpu.make_async_copy(source, target, sem.at[1 + place])
         for place, (source, target) in enumerate(
             [
-                (first_grad, first_out),
-                (second_grad, second_out),
                 (block_in, block_out),
                 (grad_in, grad_out),
+                (second_grad, second_out),
+                (first_grad, first_out),
+                (first_bias_grad, first_bias_out),
+                (second_bias_grad, second_bias_out),
+                (embed_grad, embed_out),
             ]
         )
     ]
     load.start()
+    writes[0].start()
+    writes[1].start()
+    second_grad[...] = dot(hidden[...], owned[...], TN)
     writes[2].start()
+    first_grad[...] = dot(embedding[...], pre[...], TN)
     writes[3].start()
-    second_grad[...] = dot(hidden[...], owned[...], TN)
-    writes[1].start()
-    first_grad[...] = dot(embedding[...], pre[...], TN)
-    writes[0].start()
     first_bias_grad[...] = jnp.sum(pre[...].astype(F32), axis=0)
+    writes[4].start()
     second_bias_grad[...] = jnp.sum(owned[...].astype(F32), axis=0)
+    writes[5].start()
     load.wait()
     embed_grad[...] = dot(pre[...], first_weight[...], NT)[:PREFIX]
+    writes[6].start()
     for write in writes:
         write.wait()
 
@@ -695,12 +716,15 @@
             jax.ShapeDtypeStruct((owned,), F32),
         ),
         in_specs=[local] * 6 + [anywhere],
-        out_specs=[anywhere, anywhere, local, anywhere, local, anywhere, local],
+        out_specs=[anywhere] * 7,
         scratch_shapes=[
             pltpu.VMEM((width, hidden_width), BF16),
             pltpu.VMEM((width, hidden_width), F32),
             pltpu.VMEM((hidden_width, owned), F32),
-            dma((5,)),
+            pltpu.VMEM((hidden_width,), F32),
+            pltpu.VMEM((owned,), F32),
+            pltpu.VMEM((PREFIX, width), F32),
+            dma((8,)),
         ],
         compiler_params=pltpu.CompilerParams(vmem_limit_bytes=16 * 2**20),
         name="small_grads",

time: 89.7 us -> 87.5 us (0.975)
  Pallas kernels: 87.4 us -> 85.2 us
    pallas_call x1, Pallas kernels: 83.7 us -> 82.1 us  [shards(): pl.pallas_call(functools.partial(layer_kernel, dp_size, col_size), out_sh...]
where the time goes in v2:
time: 87.5 us; the launch traced here: 87.3 us
  Pallas kernels  85.2 us (97%)
  local copies, waits for them, and re-layouts  1.22 us (1%)
    pallas_call x1, Pallas kernels, shards(): pl.pallas_call(functools.partial(layer_kernel, dp_size, col_size), out_sh...  82.1 us
    pallas_call x1, Pallas kernels, shards(): pl.pallas_call(small_kernel, out_shape=(jax.ShapeDtypeStruct((row_count,...  3.16 us

profile of v2, /device:TPU:0, one launch (start us, length us, event | category | flops | bytes accessed | tf_op | source)
XLA Modules:
  0.0 87.3 jit_solution(1786804147898954224)
XLA Ops:
  0.6 82.1 %layer.1 = (bf16[1024,1024]{1,0:T(8,128)(2,1)S(1)}, bf16[1024,1024]{1,0:T(8,128)(2,1)S(1)}, bf16[16,512]{1,0:T(8,128)(2,1)S(1)}, bf16[16,512]{1,0:T(8,128)(2,1)S...) custom-call(bf16[1024,1024]{1,0:T(8,128)(2,1)} %tokens_hbm.1, bf16[1024,1024]{1,0:T(8,128)(2,1)} %cotangent_hbm.1, ...), custom_call_target="tpu_custom_call" | custom-call | tf_op jit(solution)/shard_map/layer/pallas_call | solution.py:639
  82.7 0.0 copy-start
  82.7 1.2 %copy-done = bf16[1024,512]{1,0:T(8,128)(2,1)S(1)} copy-done((bf16[1024,512]{1,0:T(8,128)(2,1)S(1)}, bf16[1024,512]{1,0:T(8,128)(2,1)}, u32[]{:S(2)}) %copy-start) | copy-done | bytes 1048600
  84.0 3.2 %small_grads.1 = (bf16[1024,1024]{1,0:T(8,128)(2,1)}, bf16[1024,1024]{1,0:T(8,128)(2,1)}, f32[10,1024]{1,0:T(8,128)}, f32[1024,512]{1,0:T(8,128)}, f32[512]{0:T(512)}, /*index=5*/f32[512,512]{1,0:T(8,128)}, f32[512]{0:T(512)}) custom-call(bf16[1024,1024]{1,0:T(8,128)(2,1)S(1)} %get-tuple-element.13.block_in, ...), custom_call_target="tpu_custom_call" | custom-call | tf_op jit(solution)/shard_map/small_grads/pallas_call | solution.py:707
Async XLA Ops:
  82.7 1.2 %copy-start = (bf16[1024,512]{1,0:T(8,128)(2,1)S(1)}, bf16[1024,512]{1,0:T(8,128)(2,1)}, u32[]{:S(2)}) copy-start(bf16[1024,512]{1,0:T(8,128)(2,1)} %first_hbm.3) | copy-start | bytes 3145732

commit v3 on v2

--- a/solution.py
+++ b/solution.py
@@ -103,7 +103,7 @@
     ]
 
 
-def attention_forward(seq, width, packed, prefix, attended, top, bottom, side):
+def attention_forward(seq, width, packed, prefix, attended, top, bottom, side, norms):
     rows = pl.ds(pl.multiple_of(seq * SEQ_LEN, SEQ_LEN), SEQ_LEN)
     pairs = width // PAIR
     key = lax.broadcasted_iota(jnp.int32, (HALF, HALF), 0)
@@ -145,35 +145,30 @@
             + total[:, HALF:]
         )
         inverse = 1.0 / jnp.concatenate([total_early, total_late], axis=1)
-        first = jnp.concatenate(
-            [
-                (early * inverse[:, :HALF]).astype(BF16),
-                (cross * inverse[:, HALF:]).astype(BF16),
-            ],
-            axis=1,
-        )
-        probs.append(
-            (first, (late * inverse[:, HALF:]).astype(BF16), (extra * inverse).astype(BF16))
-        )
+        first = jnp.concatenate([early.astype(BF16), cross.astype(BF16)], axis=1)
+        probs.append((first, late.astype(BF16), extra.astype(BF16), inverse))
     empty = jnp.zeros((HALF, HALF), BF16)
     for pair in range(pairs):
         values = packed[rows, columns(2 * width, pair)].T
         prefix_values = prefix[:, columns(width, pair)].T
         halves = []
         for head in (0, 1):
-            first, second, extra = probs[2 * pair + head]
+            first, second, extra, inverse = probs[2 * pair + head]
             place = seq * HEADS + 2 * pair + head
             top[place] = first
             bottom[place] = second
             side[place] = extra
+            norms[pl.ds(place, 1), :] = inverse
             whole = jnp.concatenate([first, jnp.concatenate([empty, second], axis=1)], axis=0)
             mine = slice(head * (PAIR // 2), (head + 1) * (PAIR // 2))
-            halves.append(dot(values[mine], whole) + dot(prefix_values[mine], extra))
+            halves.append(
+                (dot(values[mine], whole) + dot(prefix_values[mine], extra)) * inverse
+            )
         attended[rows, columns(0, pair)] = jnp.concatenate(halves, axis=0).astype(BF16).T
 
 
 def attention_backward(
-    seq, width, packed, prefix, upstream, attended, top, bottom, side, prefix_grad
+    seq, width, packed, prefix, upstream, attended, top, bottom, side, norms, prefix_grad
 ):
     rows = pl.ds(pl.multiple_of(seq * SEQ_LEN, SEQ_LEN), SEQ_LEN)
     pairs = width // PAIR
@@ -191,22 +186,28 @@
                 packed[rows, columns(2 * width, pair)], prefix[:, columns(width, pair)], grad, lanes
             )
         )
-    slopes = []
+    slopes, probs = [], []
     for pair in range(pairs):
         for head in (0, 1):
             place = seq * HEADS + 2 * pair + head
             first, second, extra = incoming[pair][head]
             delta = deltas[pair][head : head + 1, :]
-            first = (top[place].astype(F32) * (first - delta)).astype(BF16)
-            second = (bottom[place].astype(F32) * (second - delta[:, HALF:])).astype(BF16)
-            extra = (side[place].astype(F32) * (extra - delta)).astype(BF16)
+            inverse = norms[pl.ds(place, 1), :]
+            chances = [
+                top[place].astype(F32) * inverse,
+                bottom[place].astype(F32) * inverse[:, HALF:],
+                side[place].astype(F32) * inverse,
+            ]
+            first = (chances[0] * (first - delta)).astype(BF16)
+            second = (chances[1] * (second - delta[:, HALF:])).astype(BF16)
+            extra = (chances[2] * (extra - delta)).astype(BF16)
             slopes.append((first, second, extra))
+            probs.append([part.astype(BF16) for part in chances])
     for pair in range(pairs):
         grad = upstream[rows, columns(0, pair)]
         queries = packed[rows, columns(0, pair)]
         keys = packed[rows, columns(width, pair)].T
         prefix_keys = prefix[:, columns(0, pair)].T
-        place = seq * HEADS + 2 * pair
 
         def pulled(stream, first, second, extra):
             masked = [jnp.where(mine, stream, 0) for mine in lanes]
@@ -223,9 +224,7 @@
         )
         value_first, value_second, value_extra = pulled(
             grad,
-            (top[place], top[place + 1]),
-            (bottom[place], bottom[place + 1]),
-            (side[place], side[place + 1]),
+            *zip(probs[2 * pair], probs[2 * pair + 1]),
         )
         halves = []
         for head in (0, 1):
@@ -282,6 +281,7 @@
     top,
     bottom,
     side,
+    norms,
     middle,
     normed,
     activated,
@@ -393,7 +393,7 @@
         gather.wait()
 
     def forward_step(seq, carry):
-        attention_forward(seq, width, packed, prefix, attended, top, bottom, side)
+        attention_forward(seq, width, packed, prefix, attended, top, bottom, side, norms)
         return carry
 
     lax.fori_loop(0, seqs, forward_step, 0)
@@ -452,7 +452,7 @@
 
     def backward_step(seq, carry):
         attention_backward(
-            seq, width, packed, prefix, normed, attended, top, bottom, side, prefix_grad
+            seq, width, packed, prefix, normed, attended, top, bottom, side, norms, prefix_grad
         )
         return carry
 
@@ -657,6 +657,7 @@
             pltpu.VMEM((heads, HALF, SEQ_LEN), BF16),
             pltpu.VMEM((heads, HALF, HALF), BF16),
             pltpu.VMEM((heads, PAD, SEQ_LEN), BF16),
+            pltpu.VMEM((heads, SEQ_LEN), F32),
             pltpu.VMEM((row_count, width), BF16),
             pltpu.VMEM((row_count, width), BF16),
             pltpu.VMEM((max(row_count, width), ff), BF16),

time: 87.5 us -> 87.3 us (level)
  no operation moved by 1% of the time
where the time goes in v3:
time: 87.3 us; the launch traced here: 87.1 us
  Pallas kernels  85 us (97%)
  local copies, waits for them, and re-layouts  1.22 us (1%)
    pallas_call x1, Pallas kernels, shards(): pl.pallas_call(functools.partial(layer_kernel, dp_size, col_size), out_sh...  81.9 us
    pallas_call x1, Pallas kernels, shards(): pl.pallas_call(small_kernel, out_shape=(jax.ShapeDtypeStruct((row_count,...  3.16 us

profile of v3, /device:TPU:0, one launch (start us, length us, event | category | flops | bytes accessed | tf_op | source)
XLA Modules:
  0.0 87.1 jit_solution(315042373030580191)
XLA Ops:
  0.6 81.9 %layer.1 = (bf16[1024,1024]{1,0:T(8,128)(2,1)S(1)}, bf16[1024,1024]{1,0:T(8,128)(2,1)S(1)}, bf16[16,512]{1,0:T(8,128)(2,1)S(1)}, bf16[16,512]{1,0:T(8,128)(2,1)S...) custom-call(bf16[1024,1024]{1,0:T(8,128)(2,1)} %tokens_hbm.1, bf16[1024,1024]{1,0:T(8,128)(2,1)} %cotangent_hbm.1, ...), custom_call_target="tpu_custom_call" | custom-call | tf_op jit(solution)/shard_map/layer/pallas_call | solution.py:639
  82.5 0.0 copy-start
  82.5 1.2 %copy-done = bf16[1024,512]{1,0:T(8,128)(2,1)S(1)} copy-done((bf16[1024,512]{1,0:T(8,128)(2,1)S(1)}, bf16[1024,512]{1,0:T(8,128)(2,1)}, u32[]{:S(2)}) %copy-start) | copy-done | bytes 1048600
  83.7 3.2 %small_grads.1 = (bf16[1024,1024]{1,0:T(8,128)(2,1)}, bf16[1024,1024]{1,0:T(8,128)(2,1)}, f32[10,1024]{1,0:T(8,128)}, f32[1024,512]{1,0:T(8,128)}, f32[512]{0:T(512)}, /*index=5*/f32[512,512]{1,0:T(8,128)}, f32[512]{0:T(512)}) custom-call(bf16[1024,1024]{1,0:T(8,128)(2,1)S(1)} %get-tuple-element.13.block_in, ...), custom_call_target="tpu_custom_call" | custom-call | tf_op jit(solution)/shard_map/small_grads/pallas_call | solution.py:708
Async XLA Ops:
  82.5 1.2 %copy-start = (bf16[1024,512]{1,0:T(8,128)(2,1)S(1)}, bf16[1024,512]{1,0:T(8,128)(2,1)}, u32[]{:S(2)}) copy-start(bf16[1024,512]{1,0:T(8,128)(2,1)} %first_hbm.3) | copy-start | bytes 3145732
